TPU v7x, 256 devices: a whole 4x4x8 slice. The times are simulated.
256 devices in a mesh: tm: 8 (over z_lo, core), pix: 32 (over x, y, z_hi).
Axes of the slice: x: 4, y: 4, z: 8 (z_hi: 2, z_lo: 4; z = z_hi * 4 + z_lo), core: 2. Of those that a mesh axis runs over, the one named last changes fastest.
Arguments:
- frames: float32 [2048, 32768], P('tm', 'pix'), may hold values from -6 to 6
- ann_rows: int32 [256], P('pix'), may hold values from 0 to 3, as said below
- start_bases: float32 [4, 2048, 256], P(None, ('tm', 'pix')), may hold values from -0.125 to 0.125
Outputs:
- cleaned: float32 [2048, 32768], P('tm', 'pix')
Inputs may be any that keep to these rules, and one draw needn't show every extreme that they name: `ann_rows`: annulus numbers never fall along the rows; every annulus holds at least 32 rows, and one holds exactly that many.
All inputs are finite; a program needn't handle non-finite values.
Results may differ from a plain program's by a relative error of at most 0.0003.
Values sent between devices are 32-bit elements; how exact they have to be, the bound alone decides.
A program may use at most 64 MiB of HBM per device.

v0:
```python
import jax
import jax.numpy as jnp
from jax import lax
from jax.sharding import PartitionSpec as P

ITERS = 2


def orthonormal(product):
    squares = jnp.einsum("aik,ail->akl", product, product, precision=lax.Precision.HIGHEST)
    squares = lax.psum(squares, ("tm", "pix"))
    factor = jnp.linalg.cholesky(squares)
    solved = jax.scipy.linalg.solve_triangular(factor, jnp.swapaxes(product, 1, 2), lower=True)
    return jnp.swapaxes(solved, 1, 2)


def shards(frames, ann_rows, start_bases):
    highest = lax.Precision.HIGHEST
    frame_dev, pix_dev = frames.shape
    annuli, row_dev, subspace = start_bases.shape
    row_count = pix_dev // 128
    blocks = [frames[:, row * 128 : (row + 1) * 128] for row in range(row_count)]
    current = start_bases
    shard_rows = lax.all_gather(frames, "tm", axis=0, tiled=True)
    gram_partials = jnp.zeros((annuli, frame_dev, shard_rows.shape[0]), jnp.float32)
    for gram_row in range(row_count):
        theirs = shard_rows[:, gram_row * 128 : (gram_row + 1) * 128]
        gram_product = jnp.einsum("fp,gp->fg", blocks[gram_row], theirs, precision=highest)
        gram_partials = gram_partials.at[ann_rows[gram_row]].add(gram_product)
    partial_value = gram_partials
    tm_count = lax.axis_size("tm")
    partial_value = partial_value.reshape(annuli, frame_dev, tm_count, frame_dev)
    gram_block = lax.psum_scatter(partial_value, "pix", scatter_dimension=3, tiled=True)
    gram_block = gram_block.reshape(annuli, frame_dev, tm_count * row_dev)
    for sweep in range(ITERS):
        columns = lax.all_gather(current, "tm", axis=1, tiled=True)
        partials = jnp.einsum("afg,agk->afk", gram_block, columns, precision=highest)
        product = lax.psum_scatter(partials, "pix", scatter_dimension=1, tiled=True)
        current = orthonormal(product)
    last_basis = lax.all_gather(current, "pix", axis=1, tiled=True)
    coefficients = jnp.concatenate(
        [
            jnp.einsum("fk,fp->kp", last_basis[ann_rows[row]], blocks[row], precision=highest)
            for row in range(row_count)
        ],
        1,
    )
    coefficients = lax.psum(coefficients, "tm")
    cleaned = jnp.concatenate(
        [
            blocks[row]
            - jnp.dot(
                last_basis[ann_rows[row]],
                coefficients[:, row * 128 : (row + 1) * 128],
                precision=highest,
                preferred_element_type=jnp.float32,
            )
            for row in range(row_count)
        ],
        1,
    )
    return cleaned


def solution(mesh):
    placed = (P("tm", "pix"), P("pix"), P(None, ("tm", "pix"), None))
    return jax.shard_map(
        shards, mesh=mesh, in_specs=placed, out_specs=P("tm", "pix"), check_vma=False
    )
```

profile of v0, /device:TPU:1, one launch (start us, length us, event | category | flops | bytes accessed | tf_op | source)
XLA Modules:
  0.0 2133.6 jit_solution(4736687861266342086)
XLA Ops:
  27.1 77.6 %all-gather.3.cloned.1.call-done = f32[2048,1024]{1,0:T(8,128)} async-done(((f32[256,1024]{1,0:T(8,128)}), f32[2048,1024]{1,0:T(8,128)}) %all-gather.3.cloned.1.call-update) | async-done | bytes 8388624 | tf_op jit(solution)/shard_map/all_gather | solution.py:24
  110.5 2.6 fusion.2
  113.1 2.7 fusion.3
  115.8 2.6 fusion.4
  118.4 2.6 fusion.5
  121.0 3.2 fusion.6
  124.2 2.6 fusion.7
  126.8 2.6 fusion.8
  129.4 7.3 copy.126
  136.7 10.5 copy.83
  148.0 17.2 all_gather.13
  165.2 357.2 %reduce-scatter.4.cloned.1.call-done = f32[4,256,8,8]{1,2,0,3:T(8,128)} async-done(((f32[4,256,8,256]{1,2,0,3:T(8,128)}), f32[4,256,8,8]{1,2,0,3:T(8,128)}) %reduce-scatter.4.cloned.1.call-update) | async-done | bytes 262160 | tf_op jit(solution)/shard_map/reduce_scatter | solution.py:33
  522.4 3.0 fusion.57
  525.5 203.1 %reduce-scatter.6.cloned.1.call-done = f32[4,8,256]{2,1,0:T(8,128)} async-done(((f32[4,256,256]{2,1,0:T(8,128)}), f32[4,8,256]{2,1,0:T(8,128)}) %reduce-scatter.6.cloned.1.call-update) | async-done | bytes 32784 | tf_op jit(solution)/shard_map/reduce_scatter | solution.py:38
  728.6 2.8 fusion.123
  731.8 275.3 %all-reduce.5.cloned.1.call-done = f32[4,256,256]{1,2,0:T(8,128)} async-done(((f32[4,256,256]{1,2,0:T(8,128)}), f32[4,256,256]{1,2,0:T(8,128)}) %all-reduce.5.cloned.1.call-update) | async-done | bytes 1048592 | tf_op jit(solution)/shard_map/psum | solution.py:11
  1011.0 46.9 %custom-call.17 = f32[4,128,128]{2,1,0:T(8,128)S(1)} custom-call(f32[4,128,128]{2,1,0:T(8,128)S(1)} %cholesky.198), custom_call_target="Cholesky" | custom-call | tf_op jit(solution)/shard_map/jit(cholesky)/cholesky | solution.py:12
  1058.0 39.3 %custom-call.18 = f32[4,1,128,128]{2,3,1,0:T(8,128)S(1)} custom-call(f32[4,1,128,128]{3,2,1,0:T(8,128)S(1)} %select_bitcast_fusion.1), custom_call_target="InvertDiagBlocksLowerTriangular" | custom-call | tf_op jit(solution)/shard_map/jit(cholesky)/cholesky | solution.py:12
  1100.3 46.9 %custom-call.19 = f32[4,128,128]{2,1,0:T(8,128)S(1)} custom-call(f32[4,128,128]{2,1,0:T(8,128)S(1)} %convolution_subtract_fusion.1), custom_call_target="Cholesky" | custom-call | tf_op jit(solution)/shard_map/jit(cholesky)/cholesky | solution.py:12
  1147.7 4.2 while.12
  1152.0 79.0 %custom-call.20 = f32[4,2,128,128]{2,3,1,0:T(8,128)S(1)} custom-call(f32[4,2,128,128]{3,2,1,0:T(8,128)S(1)} %bitcast.198), custom_call_target="InvertDiagBlocksLowerTriangular" | custom-call | tf_op jit(solution)/shard_map/jit(_solve_triangular)/vmap()/triangular_solve | solution.py:13
  1232.2 16.4 all_gather.14
  1250.8 200.3 %reduce-scatter.8.cloned.1.call-done = f32[4,8,256]{2,1,0:T(8,128)} async-done(((f32[4,256,256]{2,1,0:T(8,128)}), f32[4,8,256]{2,1,0:T(8,128)}) %reduce-scatter.8.cloned.1.call-update) | async-done | bytes 32784 | tf_op jit(solution)/shard_map/reduce_scatter | solution.py:38
  1451.1 2.8 fusion.124
  1454.1 274.7 %all-reduce.7.cloned.1.call-done = f32[4,256,256]{1,2,0:T(8,128)} async-done(((f32[4,256,256]{1,2,0:T(8,128)}), f32[4,256,256]{1,2,0:T(8,128)}) %all-reduce.7.cloned.1.call-update) | async-done | bytes 1048592 | tf_op jit(solution)/shard_map/psum | solution.py:11
  1732.7 46.9 %custom-call.21 = f32[4,128,128]{2,1,0:T(8,128)S(1)} custom-call(f32[4,128,128]{2,1,0:T(8,128)S(1)} %cholesky.201), custom_call_target="Cholesky" | custom-call | tf_op jit(solution)/shard_map/jit(cholesky)/cholesky | solution.py:12
  1779.7 39.3 %custom-call.22 = f32[4,1,128,128]{2,3,1,0:T(8,128)S(1)} custom-call(f32[4,1,128,128]{3,2,1,0:T(8,128)S(1)} %select_bitcast_fusion), custom_call_target="InvertDiagBlocksLowerTriangular" | custom-call | tf_op jit(solution)/shard_map/jit(cholesky)/cholesky | solution.py:12
  1822.0 46.9 %custom-call.23 = f32[4,128,128]{2,1,0:T(8,128)S(1)} custom-call(f32[4,128,128]{2,1,0:T(8,128)S(1)} %convolution_subtract_fusion), custom_call_target="Cholesky" | custom-call | tf_op jit(solution)/shard_map/jit(cholesky)/cholesky | solution.py:12
  1869.5 4.2 while.13
  1873.7 78.8 %custom-call.24 = f32[4,2,128,128]{2,3,1,0:T(8,128)S(1)} custom-call(f32[4,2,128,128]{3,2,1,0:T(8,128)S(1)} %bitcast.197), custom_call_target="InvertDiagBlocksLowerTriangular" | custom-call | tf_op jit(solution)/shard_map/jit(_solve_triangular)/vmap()/triangular_solve | solution.py:13
  1954.4 81.0 %all-gather.5.cloned.1.call-done = f32[4,256,256]{2,1,0:T(8,128)} async-done(((f32[4,8,256]{2,1,0:T(8,128)}), f32[4,256,256]{2,1,0:T(8,128)}) %all-gather.5.cloned.1.call-update) | async-done | bytes 1048592 | tf_op jit(solution)/shard_map/all_gather | solution.py:40
  2048.3 66.4 %all-reduce.9.cloned.1.call-done = f32[256,1024]{0,1:T(8,128)} async-done(((f32[256,1024]{0,1:T(8,128)}), f32[256,1024]{0,1:T(8,128)}) %all-reduce.9.cloned.1.call-update) | async-done | bytes 1048592 | tf_op jit(solution)/shard_map/psum | solution.py:48
  (118 shorter events, 65.2 us)
Async XLA Ops:
  6.5 99.2 %copy-start.1 = (f32[256,1024]{1,0:T(8,128)S(1)}, f32[256,1024]{1,0:T(8,128)}, u32[]{:S(2)}) copy-start(f32[256,1024]{1,0:T(8,128)} %param.22) | copy-start | bytes 3145732
  6.5 98.1 %all-gather.3.cloned.1.call-start = ((), (), s32[]{:S(2)}) async-start(), calls=%async_computation.3 | async-start | bytes 9437184 | tf_op jit(solution)/shard_map/all_gather | solution.py:24
  7.3 515.2 %reduce-scatter.4.cloned.1.call-start = ((), (), s32[]{:S(2)}) async-start(), calls=%async_computation.4 | async-start | bytes 8650752 | tf_op jit(solution)/shard_map/reduce_scatter | solution.py:33
  104.6 3.4 copy-start.2
  147.2 0.8 copy-start.9
  147.3 581.3 %reduce-scatter.6.cloned.1.call-start = ((), (), s32[]{:S(2)}) async-start(), calls=%async_computation.5 | async-start | bytes 1081344 | tf_op jit(solution)/shard_map/reduce_scatter | solution.py:38
  525.5 481.6 %all-reduce.5.cloned.1.call-start = ((), (), s32[]{:S(2)}) async-start(), calls=%async_computation.6 | async-start | bytes 2097152 | tf_op jit(solution)/shard_map/psum | solution.py:11
  731.4 499.6 %copy-start.7 = (f32[4,8,256]{2,1,0:T(8,128)S(1)}, f32[4,8,256]{2,1,0:T(8,128)}, u32[]{:S(2)}) copy-start(f32[4,8,256]{2,1,0:T(8,128)} %reduce-scatter.6.cloned.1.call-done) | copy-start | bytes 98308
  731.4 719.7 %reduce-scatter.8.cloned.1.call-start = ((), (), s32[]{:S(2)}) async-start(), calls=%async_computation.7 | async-start | bytes 1081344 | tf_op jit(solution)/shard_map/reduce_scatter | solution.py:38
  731.8 516.9 %copy-start.6 = (f32[4,256,8,8]{1,2,0,3:T(8,128)S(1)}, f32[4,256,8,8]{1,2,0,3:T(8,128)}, u32[]{:S(2)}) copy-start(f32[4,256,8,8]{1,2,0,3:T(8,128)} %reduce-scatter.4.cloned.1.call-done) | copy-start | bytes 786436
  1010.0 1.0 copy-start.4
  1250.7 478.0 %all-reduce.7.cloned.1.call-start = ((), (), s32[]{:S(2)}) async-start(), calls=%async_computation.8 | async-start | bytes 2097152 | tf_op jit(solution)/shard_map/psum | solution.py:11
  1454.0 498.5 %copy-start.8 = (f32[4,8,256]{2,1,0:T(8,128)S(1)}, f32[4,8,256]{2,1,0:T(8,128)}, u32[]{:S(2)}) copy-start(f32[4,8,256]{2,1,0:T(8,128)} %reduce-scatter.8.cloned.1.call-done) | copy-start | bytes 98308
  1454.0 581.4 %all-gather.5.cloned.1.call-start = ((), (), s32[]{:S(2)}) async-start(), calls=%async_computation.9 | async-start | bytes 1081344 | tf_op jit(solution)/shard_map/all_gather | solution.py:40
  1731.7 1.0 copy-start.3
  1954.3 160.4 %all-reduce.9.cloned.1.call-start = ((), (), s32[]{:S(2)}) async-start(), calls=%async_computation.10 | async-start | bytes 2097152 | tf_op jit(solution)/shard_map/psum | solution.py:48
  2035.4 79.3 %copy-start = (f32[4,256,256]{2,1,0:T(8,128)S(1)}, f32[4,256,256]{2,1,0:T(8,128)}, u32[]{:S(2)}) copy-start(f32[4,256,256]{2,1,0:T(8,128)} %all-gather.5.cloned.1.call-done) | copy-start | bytes 3145732
  2046.4 1.0 copy-start.5
Sparse Core Ops, SparseCore 0:
  9.1 95.4 all-gather.2
  147.4 375.0 reduce-scatter.3
  525.6 202.9 reduce-scatter.5
  734.7 272.2 all-reduce.4
  1250.9 200.2 reduce-scatter.7
  1457.3 271.4 all-reduce.6
  1954.5 80.9 all-gather.4
  2047.5 67.1 all-reduce.8
where the time goes:
time: 2150 us; the launch traced here: 2130 us
  waiting for transfers between devices  1540 us (72%)
  other arithmetic  431 us (20%)
  matrix products  61.8 us (3%)
  local copies, waits for them, and re-layouts  40.3 us (2%)
  blocking collectives  33.7 us (2%)
  between operations  29.5 us (1%)
    psum x2, waiting for transfers between devices, orthonormal(): squares = lax.psum(squares, ('tm', 'pix'))  550 us
    reduce_scatter x2, waiting for transfers between devices, shards(): product = lax.psum_scatter(partials, 'pix', scatter_dimension=1, tiled=True)  403 us
    reduce_scatter x1, waiting for transfers between devices, shards(): lax.psum_scatter(partial_value, 'pix', scatter_dimension=3, tiled=True)  357 us
    another operation x17, other arithmetic, orthonormal(): factor = jnp.linalg.cholesky(squares)  267 us
    another operation x6, other arithmetic, orthonormal(): jax.scipy.linalg.solve_triangular(factor, jnp.swapaxes(product, 1, 2), lo...  158 us
    all_gather x1, waiting for transfers between devices, shards(): last_basis = lax.all_gather(current, 'pix', axis=1, tiled=True)  81 us
    all_gather x1, waiting for transfers between devices, shards(): shard_rows = lax.all_gather(frames, 'tm', axis=0, tiled=True)  77.6 us
    psum x1, waiting for transfers between devices, shards(): coefficients = lax.psum(coefficients, 'tm')  66.4 us
  transfers between devices with their start and end apart: 8, of which 8 were waited for; matrix products, arithmetic and copies ran while one was open for 0% of the time, Pallas kernels for 0%

commit v1 on v0

v1 whole, which is shorter than its diff:
```python
import jax
import jax.numpy as jnp
from jax import lax
from jax.experimental import pallas as pl
from jax.experimental.pallas import tpu as pltpu
from jax.sharding import PartitionSpec as P

MESH = pl.DeviceIdType.MESH
F32 = jnp.float32
BF16 = jnp.bfloat16
HIGHEST = lax.Precision.HIGHEST
ANN = 4
K = 256
NPL = 16
NN = (((1,), (0,)), ((), ()))
NT = (((1,), (1,)), ((), ()))


def dot(a, b, dims=NN):
    return lax.dot_general(a, b, dims, preferred_element_type=F32)


def dot_full(a, b, dims=NN):
    return lax.dot_general(a, b, dims, precision=HIGHEST, preferred_element_type=F32)


def split(a):
    high = a.astype(BF16)
    return high, (a - high.astype(F32)).astype(BF16)


def dot3(ah, al, bh, bl, dims=NN):
    return dot(ah, bh, dims) + (dot(ah, bl, dims) + dot(al, bh, dims))


def leaf(a):
    n = 128
    groups = n // 8
    sub = lax.broadcasted_iota(jnp.int32, (8, n), 0)
    lane = lax.broadcasted_iota(jnp.int32, (8, n), 1)
    left = [a[8 * g : 8 * g + 8, :] for g in range(groups)]
    right = [jnp.where(lane == sub + 8 * g, 1.0, 0.0).astype(F32) for g in range(groups)]
    for k in range(n):
        g0, k0 = k // 8, k % 8
        columns = [jnp.broadcast_to(left[g][:, k : k + 1], (8, n)) for g in range(g0, groups)]
        pivot = columns[0][k0 : k0 + 1, :]
        inverse = 1.0 / pivot
        row_left = left[g0][k0 : k0 + 1, :] * inverse
        row_right = right[g0][k0 : k0 + 1, :] * inverse
        scale = lax.rsqrt(pivot)
        for g in range(g0, groups):
            column = columns[g - g0]
            if g == g0:
                column = jnp.where(sub > k0, column, 0.0)
            left[g] = left[g] - column * row_left
            right[g] = right[g] - column * row_right
        right[g0] = jnp.where(sub == k0, right[g0] * scale, right[g0])
    return jnp.concatenate(right, 0)


def inverse_factor(s_ref, out_ref):
    first = leaf(s_ref[0:128, 0:128])
    out_ref[0:128, 0:128] = first
    out_ref[0:128, 128:256] = jnp.zeros((128, 128), F32)
    lower = dot_full(s_ref[128:256, 0:128], first, NT)
    second = leaf(s_ref[128:256, 128:256] - dot_full(lower, lower, NT))
    out_ref[128:256, 128:256] = second
    out_ref[128:256, 0:128] = -dot_full(second, dot_full(lower, out_ref[0:128, 0:128]))


def kernel(
    frames, ids, base, out,
    xw, xh, xl, xth, xtl, bs, bh, bl, zb,
    own, erecv, mrecv, tot, ymh, yml,
    pbuf, prec, rsend, rrecv, st, zrecv, gbuf, idtile, idall,
    smat, linv, y3, ot,
    core_send, core_recv, plane_send, plane_recv, zsend, zrec, line_send, line_recv,
):
    t, p = lax.axis_index("tm"), lax.axis_index("pix")
    c, zl = lax.rem(t, 2), t // 2
    q, zh = p // 2, lax.rem(p, 2)
    is_mid = jnp.logical_or(zl == 1, zl == 2)
    is_end = jnp.logical_or(zl == 0, zl == 3)
    other = {"tm": t + 1 - 2 * c, "pix": p}
    across = {"tm": t, "pix": 2 * q + 1 - zh}
    pair = {"tm": 2 * (zl + 1 - 2 * lax.rem(zl, 2)) + c, "pix": p}
    middle = {"tm": 2 * (3 - zl) + c, "pix": p}

    def peer(d):
        return {"tm": t, "pix": 2 * d + zh}

    def remote(src, dst, send, recv, device):
        return pltpu.make_async_remote_copy(
            src_ref=src, dst_ref=dst, send_sem=send, recv_sem=recv, device_id=device, device_id_type=MESH
        )

    def greet(device):
        pl.semaphore_signal(barrier, inc=1, device_id=device, device_id_type=MESH)

    def each_peer(body):
        def step(d, _):
            body(lax.rem(q + d, NPL))
            return 0

        lax.fori_loop(1, NPL, step, 0)

    barrier = pltpu.get_barrier_semaphore()
    greet(other)
    greet(across)
    greet(pair)
    each_peer(lambda d: greet(peer(d)))

    @pl.when(is_mid)
    def _():
        greet(middle)

    first_id, last_id = ids[0], ids[7]
    idtile[0:1, :] = jnp.full((1, K), first_id, jnp.int32)
    idtile[1:2, :] = jnp.full((1, K), last_id, jnp.int32)
    idtile[2:8, :] = jnp.zeros((6, K), jnp.int32)
    idall[q] = idtile[...]
    pl.semaphore_wait(barrier, jnp.where(is_mid, 19, 18))

    def x_copy(side):
        return remote(
            frames.at[:, pl.ds(pl.multiple_of((1 - c) * 512, 128), 512)],
            xw.at[pl.ds(pl.multiple_of(side * 256, 256), 256), :],
            core_send.at[0], core_recv.at[0], other,
        )

    def id_copy(d, src):
        return remote(idtile, idall.at[src], plane_send.at[0, d], plane_recv.at[0, src], peer(d))

    def z_copy(phase):
        if phase == 0:
            rows = pl.ds(pl.multiple_of(8 * zh, 8), 8)
            theirs = pl.ds(pl.multiple_of(8 * (1 - zh), 8), 8)
            return (
                remote(base, st.at[0, :, rows, :], zsend.at[0], zrec.at[0], across),
                remote(base, st.at[0, :, theirs, :], zsend.at[0], zrec.at[0], across),
            )
        both = remote(st.at[phase], zrecv.at[phase - 1], zsend.at[phase], zrec.at[phase], across)
        return both, both

    def g_copy(phase, d, src):
        return remote(
            gbuf.at[phase, d],
            bs.at[phase, :, pl.ds(pl.multiple_of(c * 256 + src * 16, 16), 16), :],
            plane_send.at[1 + phase, d], plane_recv.at[1 + phase, src], peer(d),
        )

    def half_copy(phase, side):
        rows = pl.ds(pl.multiple_of(side * 256, 256), 256)
        return remote(
            bs.at[phase, :, rows, :], bs.at[phase, :, rows, :],
            core_send.at[1 + phase], core_recv.at[1 + phase], other,
        )

    def p_copy(phase):
        rows = pl.ds(pl.multiple_of((1 - c) * 256, 256), 256)
        return remote(
            pbuf.at[phase, :, rows, :], prec.at[phase], core_send.at[4 + phase], core_recv.at[4 + phase], other
        )

    def r_copy(phase, d, src):
        return remote(
            rsend.at[phase, :, pl.ds(pl.multiple_of(d * 16, 16), 16), :],
            rrecv.at[phase, src],
            plane_send.at[4 + phase, d], plane_recv.at[4 + phase, src], peer(d),
        )

    def end_copy(phase, ch):
        return remote(own.at[phase, ch], erecv.at[phase, ch], line_send.at[phase, 0, ch], line_recv.at[phase, 0, ch], pair)

    def mid_copy(phase, ch):
        return remote(
            own.at[phase, ch], mrecv.at[phase, ch], line_send.at[phase, 1, ch], line_recv.at[phase, 1, ch], middle
        )

    def total_copy(phase, ch):
        return remote(tot.at[phase, ch], tot.at[phase, ch], line_send.at[phase, 2, ch], line_recv.at[phase, 2, ch], pair)

    def factor_copy(which, slot):
        return remote(
            linv.at[which, slot], linv.at[which, slot], core_send.at[6 + which], core_recv.at[6 + which], other
        )

    def y_copy(side):
        rows = pl.ds(pl.multiple_of(side * 4, 4), 4)
        return remote(y3.at[rows], y3.at[rows], core_send.at[8], core_recv.at[8], other)

    x_copy(c).start()
    z_copy(0)[0].start()
    each_peer(lambda d: id_copy(d, q).start())
    st[0, :, pl.ds(pl.multiple_of(8 * zh, 8), 8), :] = base[...]
    xw[pl.ds(pl.multiple_of(c * 256, 256), 256), :] = frames[:, pl.ds(pl.multiple_of(c * 512, 128), 512)]

    def slot_of(row):
        return jnp.where(ids[row] == first_id, 0, 1)

    def share(phase):
        def fill(d, _):
            for s in range(2):
                which = idall[d, s : s + 1, :]
                value = jnp.zeros((16, K), F32)
                for a in range(ANN):
                    value = jnp.where(which == a, st[phase, a], value)
                gbuf[phase, d, s] = value
            return 0

        lax.fori_loop(0, NPL, fill, 0)
        each_peer(lambda d: g_copy(phase, d, q).start())
        bs[phase, :, pl.ds(pl.multiple_of(c * 256 + q * 16, 16), 16), :] = gbuf[phase, q]
        each_peer(lambda d: g_copy(phase, d, d).wait_recv())
        half_copy(phase, c).start()
        half_copy(phase, 1 - c).wait_recv()

    def line_sum(phase, count):
        @pl.when(is_mid)
        def _():
            def meet(ch, _):
                end_copy(phase, ch).wait_recv()
                own[phase, ch] = own[phase, ch] + erecv[phase, ch]
                mid_copy(phase, ch).start()
                return 0

            def finish(ch, _):
                mid_copy(phase, ch).wait_recv()
                tot[phase, ch] = own[phase, ch] + mrecv[phase, ch]
                total_copy(phase, ch).start()
                return 0

            def step(ch, _):
                meet(ch, 0)
                finish(ch - 1, 0)
                return 0

            meet(0, 0)
            lax.fori_loop(1, count, step, 0)
            finish(count - 1, 0)

        @pl.when(is_end)
        def _():
            def take(ch, _):
                total_copy(phase, ch).wait_recv()
                return 0

            lax.fori_loop(0, count, take, 0)

    def chunk_done(phase, ch):
        @pl.when(is_end)
        def _():
            end_copy(phase, ch).start()

    def project(phase, source):
        for s in range(2):
            high, low = split(source[s])
            bh[s] = high
            bl[s] = low
        skip = 0
        if phase > 0:
            skip = 2
            mine = source[c]
            flipped = mine.T
            for half in range(2):
                own[phase, half] = dot_full(flipped[128 * half : 128 * half + 128, :], mine)
                chunk_done(phase, half)

        def chunk(r, _):
            rows = pl.ds(pl.multiple_of(r * 128, 128), 128)
            s = slot_of(4 * c + r)
            own[phase, skip + r] = dot3(xth[rows, :], xtl[rows, :], bh[s], bl[s])
            chunk_done(phase, skip + r)
            return 0

        lax.fori_loop(0, 4, chunk, 0)
        line_sum(phase, skip + 4)

    def back(phase, between):
        skip = 2 if phase > 0 else 0

        def mask(r, _):
            rows = pl.ds(pl.multiple_of(r * 128, 128), 128)
            s = slot_of(4 * c + r)
            high, low = split(tot[phase, skip + r])
            none = jnp.zeros((128, K), BF16)
            ymh[0, rows, :] = jnp.where(s == 0, high, none)
            yml[0, rows, :] = jnp.where(s == 0, low, none)
            ymh[1, rows, :] = jnp.where(s == 1, high, none)
            yml[1, rows, :] = jnp.where(s == 1, low, none)
            return 0

        lax.fori_loop(0, 4, mask, 0)

        def multiply(i, _):
            for s in range(2):
                rows = pl.ds(pl.multiple_of(i * 128, 128), 128)
                pbuf[phase, s, rows, :] = dot3(xh[rows, :], xl[rows, :], ymh[s], yml[s])
            return 0

        lax.fori_loop(0, 4, multiply, 0)
        p_copy(phase).start()
        p_copy(phase).wait_recv()
        rsend[phase] = pbuf[phase, :, pl.ds(pl.multiple_of(c * 256, 256), 256), :] + prec[phase]
        each_peer(lambda d: r_copy(phase, d, q).start())
        rrecv[phase, q] = rsend[phase, :, pl.ds(pl.multiple_of(q * 16, 16), 16), :]
        between()
        each_peer(lambda d: r_copy(phase, d, d).wait_recv())

        def add(src, sums):
            new = list(sums)
            for s in range(2):
                which = idall[src, s : s + 1, :]
                value = rrecv[phase, src, s]
                for a in range(ANN):
                    new[a] = new[a] + jnp.where(which == a, value, 0.0)
            return tuple(new)

        sums = lax.fori_loop(0, NPL, add, tuple(jnp.zeros((16, K), F32) for _ in range(ANN)))
        for a in range(ANN):
            st[phase + 1, a] = sums[a]
        z_copy(phase + 1)[0].start()
        z_copy(phase + 1)[1].wait()
        for a in range(ANN):
            st[phase + 1, a] = sums[a] + zrecv[phase, a]

    x_copy(1 - c).wait_recv()

    def layouts(i, _):
        rows = pl.ds(pl.multiple_of(i * 128, 128), 128)
        block = xw[rows, :]
        high, low = split(block)
        xh[rows, :] = high
        xl[rows, :] = low
        turned = block.T
        high, low = split(turned)
        xth[:, rows] = high
        xtl[:, rows] = low
        return 0

    lax.fori_loop(0, 4, layouts, 0)
    z_copy(0)[1].wait_recv()
    each_peer(lambda d: id_copy(d, d).wait_recv())

    share(0)
    project(0, bs.at[0])
    back(0, lambda: None)
    share(1)

    project(1, bs.at[1])

    def factor(which):
        smat[0:128, :] = tot[1 + which, 0]
        smat[128:256, :] = tot[1 + which, 1]
        inverse_factor(smat, linv.at[which, c])
        factor_copy(which, c).start()

    back(1, lambda: factor(0))
    share(2)
    factor_copy(0, 1 - c).wait_recv()

    def normalise(i, _):
        rows = pl.ds(pl.multiple_of(i * 256, 256), 256)
        for s in range(2):
            zb[s, rows, :] = dot_full(bs[2, s, rows, :], linv[0, s], NT)
        return 0

    lax.fori_loop(0, 2, normalise, 0)

    project(2, zb)
    y3[pl.ds(pl.multiple_of(c * 4, 4), 4)] = tot[2, 2:6]
    y_copy(c).start()
    factor(1)
    y_copy(1 - c).wait_recv()
    factor_copy(1, 1 - c).wait_recv()
    for s in range(2):
        basis = dot_full(zb[s, pl.ds(pl.multiple_of(c * 256, 256), 256), :], linv[1, s], NT)
        high, low = split(basis)
        bh[s, 0:256, :] = high
        bl[s, 0:256, :] = low
        high, low = split(linv[1, s])
        bh[s, 256:512, :] = high
        bl[s, 256:512, :] = low

    def clean(r, _):
        s = slot_of(r)
        high, low = split(y3[r])
        coefficients = dot3(high, low, bh[s, 256:512, :], bl[s, 256:512, :], NT)
        high, low = split(coefficients)
        columns = pl.ds(pl.multiple_of(r * 128, 128), 128)
        out[:, columns] = frames[:, columns] - dot3(bh[s, 0:256, :], bl[s, 0:256, :], high, low, NT)
        return 0

    lax.fori_loop(0, 8, clean, 0)

    x_copy(c).wait_send()
    z_copy(0)[0].wait_send()
    y_copy(c).wait_send()
    each_peer(lambda d: id_copy(d, q).wait_send())
    for phase in range(3):
        each_peer(lambda d: g_copy(phase, d, q).wait_send())
        half_copy(phase, c).wait_send()
    for phase in range(2):
        each_peer(lambda d: r_copy(phase, d, q).wait_send())
        p_copy(phase).wait_send()
        factor_copy(phase, c).wait_send()
    for phase in range(3):
        count = 6 if phase > 0 else 4

        @pl.when(is_mid)
        def _():
            def sent(ch, _):
                mid_copy(phase, ch).wait_send()
                total_copy(phase, ch).wait_send()
                return 0

            lax.fori_loop(0, count, sent, 0)

        @pl.when(is_end)
        def _():
            def sent(ch, _):
                end_copy(phase, ch).wait_send()
                return 0

            lax.fori_loop(0, count, sent, 0)


def solution(mesh):
    def step(frames, ann_rows, start_bases):
        vmem = pl.BlockSpec(memory_space=pltpu.VMEM)
        dma = pltpu.SemaphoreType.DMA
        return pl.pallas_call(
            kernel,
            out_shape=jax.ShapeDtypeStruct(frames.shape, F32),
            in_specs=[vmem, pl.BlockSpec(memory_space=pltpu.SMEM), vmem],
            out_specs=vmem,
            scratch_shapes=[
                pltpu.VMEM((512, 512), F32),
                pltpu.VMEM((512, 512), BF16),
                pltpu.VMEM((512, 512), BF16),
                pltpu.VMEM((512, 512), BF16),
                pltpu.VMEM((512, 512), BF16),
                pltpu.VMEM((3, 2, 512, K), F32),
                pltpu.VMEM((2, 512, K), BF16),
                pltpu.VMEM((2, 512, K), BF16),
                pltpu.VMEM((2, 512, K), F32),
                pltpu.VMEM((3, 6, 128, K), F32),
                pltpu.VMEM((3, 6, 128, K), F32),
                pltpu.VMEM((3, 6, 128, K), F32),
                pltpu.VMEM((3, 6, 128, K), F32),
                pltpu.VMEM((2, 512, K), BF16),
                pltpu.VMEM((2, 512, K), BF16),
                pltpu.VMEM((2, 2, 512, K), F32),
                pltpu.VMEM((2, 2, 256, K), F32),
                pltpu.VMEM((2, 2, 256, K), F32),
                pltpu.VMEM((2, NPL, 2, 16, K), F32),
                pltpu.VMEM((3, ANN, 16, K), F32),
                pltpu.VMEM((2, ANN, 16, K), F32),
                pltpu.VMEM((3, NPL, 2, 16, K), F32),
                pltpu.VMEM((8, K), jnp.int32),
                pltpu.VMEM((NPL, 8, K), jnp.int32),
                pltpu.VMEM((K, K), F32),
                pltpu.VMEM((2, 2, K, K), F32),
                pltpu.VMEM((8, 128, K), F32),
                pltpu.VMEM((8, 128), F32),
                dma((9,)), dma((9,)),
                dma((6, NPL)), dma((6, NPL)),
                dma((3,)), dma((3,)),
                dma((3, 3, 6)), dma((3, 3, 6)),
            ],
            compiler_params=pltpu.CompilerParams(
                collective_id=0, has_side_effects=True, vmem_limit_bytes=56 * 1024 * 1024
            ),
        )(frames, ann_rows, start_bases)

    return jax.shard_map(
        step,
        mesh=mesh,
        in_specs=(P("tm", "pix"), P("pix"), P(None, ("tm", "pix"), None)),
        out_specs=P("tm", "pix"),
        check_vma=False,
    )
```

time: 2150 us -> 215 us (0.10)
  waiting for transfers between devices: 1540 us -> 0 us
  other arithmetic: 431 us -> 0 us
  Pallas kernels: 0 us -> 213 us
  matrix products: 61.8 us -> 0 us
  local copies, waits for them, and re-layouts: 40.3 us -> 2.31 us
  blocking collectives: 33.7 us -> 0 us
  between operations: 29.5 us -> 0.01 us
    reduce_scatter x3 -> x0, waiting for transfers between devices: 761 us -> none  [the longest x2 403 us: shards(): product = lax.psum_scatter(partials, 'pix', scatter_dimension=1, tiled=True)]
    psum x3 -> x0, waiting for transfers between devices: 616 us -> none  [the longest x2 550 us: orthonormal(): squares = lax.psum(squares, ('tm', 'pix'))]
    another operation x25 -> x0, other arithmetic: 428 us -> none  [the longest x17 267 us: orthonormal(): factor = jnp.linalg.cholesky(squares)]
    pallas_call x0 -> x1, Pallas kernels: none -> 213 us  [step(): pl.pallas_call(kernel, out_shape=jax.ShapeDtypeStruct(frames.shape, F32),...]
    all_gather x2 -> x0, waiting for transfers between devices: 159 us -> none  [the longest x1 81 us: shards(): last_basis = lax.all_gather(current, 'pix', axis=1, tiled=True)]
    dot_general x28 -> x0, matrix products: 53.4 us -> none  [the longest x8 21.3 us: shards(): jnp.einsum('fp,gp->fg', blocks[gram_row], theirs, precision=highest)]
    all_gather x2 -> x0, blocking collectives: 33.7 us -> none  [shards(): columns = lax.all_gather(current, 'tm', axis=1, tiled=True)]
  transfers between devices with their start and end apart: 8 -> 0, of which waited for: 8 -> 0; matrix products, arithmetic and copies ran while one was open for 0% -> 0% of each run, Pallas kernels for 0% -> 0%
where the time goes in v1:
time: 215 us
  Pallas kernels  213 us (99%)
  local copies, waits for them, and re-layouts  2.31 us (1%)
    pallas_call x1, Pallas kernels, step(): pl.pallas_call(kernel, out_shape=jax.ShapeDtypeStruct(frames.shape, F32),...  213 us

profile of v1, /device:TPU:1, one launch (start us, length us, event | category | flops | bytes accessed | tf_op | source)
XLA Modules:
  0.0 215.3 jit_solution(7038558049805199063)
XLA Ops:
  0.0 212.9 %shard_map.37 = f32[256,1024]{1,0:T(8,128)} custom-call(f32[256,1024]{1,0:T(8,128)} %frames.1, s32[8]{0:T(128)} %ids.1, f32[4,8,256]{2,1,0:T(8,128)} %base.1), custom_call_target="tpu_custom_call" | custom-call | tf_op jit(solution)/shard_map/pallas_call | solution.py:432
  212.9 2.3 %copy.5 = f32[256,1024]{1,0:T(8,128)} copy(f32[256,1024]{1,0:T(8,128)} %shard_map.37) | data formatting | bytes 2097152

commit v2 on v1

v2 whole, which is shorter than its diff:
```python
import jax
import jax.numpy as jnp
from jax import lax
from jax.experimental import pallas as pl
from jax.experimental.pallas import tpu as pltpu
from jax.sharding import PartitionSpec as P

MESH = pl.DeviceIdType.MESH
F32 = jnp.float32
BF16 = jnp.bfloat16
HIGHEST = lax.Precision.HIGHEST
ANN = 4
K = 256
H = K // 2
NPL = 16
CHUNKS = 11
NN = (((1,), (0,)), ((), ()))
NT = (((1,), (1,)), ((), ()))


def dot(a, b, dims=NN):
    return lax.dot_general(a, b, dims, preferred_element_type=F32)


def dot_full(a, b, dims=NN):
    return lax.dot_general(a, b, dims, precision=HIGHEST, preferred_element_type=F32)


def split(a):
    high = a.astype(BF16)
    return high, (a - high.astype(F32)).astype(BF16)


def dot3(ah, al, bh, bl, dims=NN):
    return dot(ah, bh, dims) + (dot(ah, bl, dims) + dot(al, bh, dims))


def leaf(a, result):
    n = 128
    groups = n // 8
    sub = lax.broadcasted_iota(jnp.int32, (8, n), 0)
    lane = lax.broadcasted_iota(jnp.int32, (8, n), 1)
    left = [a[8 * g : 8 * g + 8, :] for g in range(groups)]
    right = [jnp.where(lane == sub + 8 * g, 1.0, 0.0).astype(F32) for g in range(groups)]
    done = []
    for g0 in range(groups):
        k0 = 8 * g0
        rows_left, rows_right, scaled = [], [], []
        own_left, own_right = left[g0], right[g0]
        columns = [jnp.broadcast_to(own_left[:, k0 + j : k0 + j + 1], (8, n)) for j in range(8)]
        final = jnp.zeros((8, n), F32)
        for j in range(8):
            pivot = columns[j][j : j + 1, :]
            inverse = 1.0 / pivot
            final = jnp.where(sub == j, own_right * lax.rsqrt(pivot), final)
            rows_left.append(own_left[j : j + 1, :] * inverse)
            rows_right.append(own_right[j : j + 1, :] * inverse)
            scaled.append([columns[i][j : j + 1, :] * inverse for i in range(j + 1, 8)])
            if j < 7:
                below = jnp.where(sub > j, columns[j], 0.0)
                own_left = own_left - below * rows_left[j]
                own_right = own_right - below * rows_right[j]
                for i in range(j + 1, 8):
                    columns[i] = columns[i] - below * scaled[j][i - j - 1]
        done.append(final)
        for g in range(g0 + 1, groups):
            columns = [jnp.broadcast_to(left[g][:, k0 + j : k0 + j + 1], (8, n)) for j in range(8)]
            new_left, new_right = left[g], right[g]
            for j in range(8):
                new_left = new_left - columns[j] * rows_left[j]
                new_right = new_right - columns[j] * rows_right[j]
                for i in range(j + 1, 8):
                    columns[i] = columns[i] - columns[j] * scaled[j][i - j - 1]
            left[g], right[g] = new_left, new_right
        yield
    result.append(jnp.concatenate(done, 0))


def inverse_factor(s00, s10, s11, out_ref):
    leaves = []
    yield from leaf(s00[...], leaves)
    first = leaves[0]
    out_ref[0:128, 0:128] = first
    out_ref[0:128, 128:256] = jnp.zeros((128, 128), F32)
    lower = dot_full(s10[...], first, NT)
    yield from leaf(s11[...] - dot_full(lower, lower, NT), leaves)
    second = leaves[1]
    out_ref[128:256, 128:256] = second
    out_ref[128:256, 0:128] = -dot_full(second, dot_full(lower, out_ref[0:128, 0:128]))


def advance(steps, count):
    for _ in range(count):
        next(steps, None)


def kernel(
    frames, ids, base, out,
    xw, xh, xl, xth, xtl, bs, bh, bl, zb,
    own, erecv, mrecv, tot, ymh, yml,
    pbuf, prec, rsend, rrecv, st, zrecv, gbuf, idtile, idall,
    linv, y3, base0,
    core_send, core_recv, plane_send, plane_recv, zsend, zrec, line_send, line_recv,
):
    t, p = lax.axis_index("tm"), lax.axis_index("pix")
    c, zl = lax.rem(t, 2), t // 2
    q, zh = p // 2, lax.rem(p, 2)
    is_mid = jnp.logical_or(zl == 1, zl == 2)
    is_end = jnp.logical_or(zl == 0, zl == 3)
    other = {"tm": t + 1 - 2 * c, "pix": p}
    across = {"tm": t, "pix": 2 * q + 1 - zh}
    pair = {"tm": 2 * (zl + 1 - 2 * lax.rem(zl, 2)) + c, "pix": p}
    middle = {"tm": 2 * (3 - zl) + c, "pix": p}

    def peer(d):
        return {"tm": t, "pix": 2 * d + zh}

    def remote(src, dst, send, recv, device):
        return pltpu.make_async_remote_copy(
            src_ref=src, dst_ref=dst, send_sem=send, recv_sem=recv, device_id=device, device_id_type=MESH
        )

    def greet(device):
        pl.semaphore_signal(barrier, inc=1, device_id=device, device_id_type=MESH)

    def each_peer(body):
        def step(d, _):
            body(lax.rem(q + d, NPL))
            return 0

        lax.fori_loop(1, NPL, step, 0)

    def part(index, size):
        return pl.ds(pl.multiple_of(index * size, size), size)

    barrier = pltpu.get_barrier_semaphore()
    greet(other)
    greet(across)
    greet(pair)
    each_peer(lambda d: greet(peer(d)))

    @pl.when(is_mid)
    def _():
        greet(middle)

    first_id, last_id = ids[0], ids[7]
    idtile[:, 0:H] = jnp.full((8, H), first_id, jnp.int32)
    idtile[:, H:K] = jnp.full((8, H), last_id, jnp.int32)
    idall[q] = idtile[...]
    for half in range(2):
        base0[half] = base[:, :, half * H : half * H + H]
    pl.semaphore_wait(barrier, jnp.where(is_mid, 19, 18))

    def x_copy(side):
        return remote(frames.at[:, part(1 - c, 512)], xw.at[part(side, 256), :], core_send.at[0], core_recv.at[0], other)

    def id_copy(d, src):
        return remote(idtile, idall.at[src], plane_send.at[0, d], plane_recv.at[0, src], peer(d))

    def base_copy(side):
        return remote(base0, st.at[0, :, :, part(side, 8), :], zsend.at[0], zrec.at[0], across)

    def z_copy(phase, half):
        k = 2 * phase + half - 1
        return remote(st.at[phase, half], zrecv.at[phase - 1, half], zsend.at[k], zrec.at[k], across)

    def g_copy(phase, half, d, src):
        k = 1 + 2 * phase + half
        return remote(
            gbuf.at[phase, half, d],
            bs.at[phase, half, pl.ds(pl.multiple_of(c * 256 + src * 16, 16), 16), :],
            plane_send.at[k, d], plane_recv.at[k, src], peer(d),
        )

    def half_copy(phase, half, side):
        k = 1 + 2 * phase + half
        rows = bs.at[phase, half, part(side, 256), :]
        return remote(rows, rows, core_send.at[k], core_recv.at[k], other)

    def p_copy(phase, half):
        k = 7 + 2 * phase + half
        return remote(
            pbuf.at[phase, half, part(1 - c, 256), :], prec.at[phase, half], core_send.at[k], core_recv.at[k], other
        )

    def r_copy(phase, half, d, src):
        k = 7 + 2 * phase + half
        return remote(
            rsend.at[phase, half, part(d, 16), :], rrecv.at[phase, half, src],
            plane_send.at[k, d], plane_recv.at[k, src], peer(d),
        )

    def end_copy(phase, ch):
        return remote(own.at[phase, ch], erecv.at[phase, ch], line_send.at[phase, 0, ch], line_recv.at[phase, 0, ch], pair)

    def mid_copy(phase, ch):
        return remote(
            own.at[phase, ch], mrecv.at[phase, ch], line_send.at[phase, 1, ch], line_recv.at[phase, 1, ch], middle
        )

    def total_copy(phase, ch):
        return remote(tot.at[phase, ch], tot.at[phase, ch], line_send.at[phase, 2, ch], line_recv.at[phase, 2, ch], pair)

    def factor_copy(which, slot):
        return remote(
            linv.at[which, slot], linv.at[which, slot], core_send.at[11 + which], core_recv.at[11 + which], other
        )

    def y_copy(half, side):
        rows = y3.at[half, part(side, 4)]
        return remote(rows, rows, core_send.at[13 + half], core_recv.at[13 + half], other)

    base_copy(zh).start()
    each_peer(lambda d: id_copy(d, q).start())
    x_copy(c).start()
    st[0, :, :, part(zh, 8), :] = base0[...]
    xw[part(c, 256), :] = frames[:, part(c, 512)]

    def slot_of(row):
        return jnp.where(ids[row] == first_id, 0, 1)

    def share(phase, half):
        def fill(d, _):
            which = idall[d, 0:1, :]
            value = jnp.zeros((16, K), F32)
            for a in range(ANN):
                rows = st[phase, half, a]
                value = jnp.where(which == a, jnp.concatenate([rows, rows], 1), value)
            gbuf[phase, half, d] = value
            return 0

        lax.fori_loop(0, NPL, fill, 0)
        each_peer(lambda d: g_copy(phase, half, d, q).start())
        bs[phase, half, pl.ds(pl.multiple_of(c * 256 + q * 16, 16), 16), :] = gbuf[phase, half, q]

    def shared(phase, half):
        each_peer(lambda d: g_copy(phase, half, d, d).wait_recv())
        half_copy(phase, half, c).start()

    def send_own(phase, ch):
        @pl.when(is_end)
        def _():
            end_copy(phase, ch).start()

    def relay(phase, meet, finish, take):
        @pl.when(is_mid)
        def _():
            for ch in meet:
                end_copy(phase, ch).wait_recv()
                own[phase, ch] = own[phase, ch] + erecv[phase, ch]
                mid_copy(phase, ch).start()
            for ch in finish:
                mid_copy(phase, ch).wait_recv()
                tot[phase, ch] = own[phase, ch] + mrecv[phase, ch]
                total_copy(phase, ch).start()

        @pl.when(is_end)
        def _():
            for ch in take:
                total_copy(phase, ch).wait_recv()

    def project(phase, half, source):
        high, low = split(source[...])
        bh[half] = high
        bl[half] = low

        def chunk(r, _):
            rows = part(r, 128)
            both = dot3(xth[rows, :], xtl[rows, :], bh[half], bl[half])
            own[phase, 4 * half + r] = jnp.where(slot_of(4 * c + r) == 0, both[:, 0:H], both[:, H:K])
            send_own(phase, 4 * half + r)
            return 0

        lax.fori_loop(0, 4, chunk, 0)

    def squares(phase, first, second):
        first, second = first[:, part(c, H)], second[:, part(c, H)]
        turned = second.T
        own[phase, 8] = dot_full(first.T, first)
        send_own(phase, 8)
        own[phase, 9] = dot_full(turned, first)
        send_own(phase, 9)
        own[phase, 10] = dot_full(turned, second)
        send_own(phase, 10)

    def back(phase, half):
        def mask(r, _):
            rows = part(r, 128)
            slot = slot_of(4 * c + r)
            value = tot[phase, 4 * half + r]
            high, low = split(jnp.concatenate([jnp.where(slot == 0, value, 0.0), jnp.where(slot == 1, value, 0.0)], 1))
            ymh[half, rows, :] = high
            yml[half, rows, :] = low
            return 0

        lax.fori_loop(0, 4, mask, 0)

        def multiply(i, _):
            rows = part(i, 256)
            pbuf[phase, half, rows, :] = dot3(xh[rows, :], xl[rows, :], ymh[half], yml[half])
            return 0

        lax.fori_loop(0, 2, multiply, 0)
        p_copy(phase, half).start()

    def scatter(phase, half):
        p_copy(phase, half).wait_recv()
        rsend[phase, half] = pbuf[phase, half, part(c, 256), :] + prec[phase, half]
        each_peer(lambda d: r_copy(phase, half, d, q).start())
        rrecv[phase, half, q] = rsend[phase, half, part(q, 16), :]

    def combine(phase, half):
        each_peer(lambda d: r_copy(phase, half, d, d).wait_recv())

        def add(src, sums):
            which = idall[src, 0:1, :]
            value = rrecv[phase, half, src]
            new = []
            for a in range(ANN):
                kept = jnp.where(which == a, value, 0.0)
                new.append(sums[a] + (kept[:, 0:H] + kept[:, H:K]))
            return tuple(new)

        sums = lax.fori_loop(0, NPL, add, tuple(jnp.zeros((16, H), F32) for _ in range(ANN)))
        for a in range(ANN):
            st[phase + 1, half, a] = sums[a]
        z_copy(phase + 1, half).start()

    def settle(phase, half):
        z_copy(phase, half).wait()
        st[phase, half] = st[phase, half] + zrecv[phase - 1, half]

    x_copy(1 - c).wait_recv()

    def layouts(i, _):
        rows = part(i, 128)
        block = xw[rows, :]
        high, low = split(block)
        xh[rows, :] = high
        xl[rows, :] = low
        high, low = split(block.T)
        xth[:, rows] = high
        xtl[:, rows] = low
        return 0

    lax.fori_loop(0, 4, layouts, 0)
    base_copy(1 - zh).wait_recv()
    each_peer(lambda d: id_copy(d, d).wait_recv())
    for half in range(2):
        share(0, half)

    factor = iter(())
    for phase in range(2):
        for half in range(2):
            shared(phase, half)
        for half in range(2):
            half_copy(phase, half, 1 - c).wait_recv()
            project(phase, half, bs.at[phase, half])
        relay(phase, [0, 1], [], [])
        if phase == 1:
            squares(1, bs.at[1, 0], bs.at[1, 1])
        relay(phase, [2], [0], [])
        relay(phase, [3], [1], [])
        relay(phase, [4], [2], [])
        relay(phase, [5], [3], [0, 1, 2, 3])
        back(phase, 0)
        relay(phase, [6], [4], [])
        relay(phase, [7], [5], [])
        if phase == 1:
            relay(phase, [8], [6], [])
            relay(phase, [9], [7], [4, 5, 6, 7])
        else:
            relay(phase, [], [6, 7], [4, 5, 6, 7])
        back(phase, 1)
        if phase == 1:
            relay(phase, [10], [8], [])
        scatter(phase, 0)
        if phase == 1:
            relay(phase, [], [9, 10], [])
        scatter(phase, 1)
        if phase == 1:
            relay(phase, [], [], [8, 9, 10])
            factor = inverse_factor(tot.at[1, 8], tot.at[1, 9], tot.at[1, 10], linv.at[0, c])
        advance(factor, 10)
        for half in range(2):
            combine(phase, half)
        advance(factor, 10)
        for half in range(2):
            settle(phase + 1, half)
            share(phase + 1, half)
        advance(factor, 100)
    factor_copy(0, c).start()

    for half in range(2):
        shared(2, half)
    factor_copy(0, 1 - c).wait_recv()
    for half in range(2):
        half_copy(2, half, 1 - c).wait_recv()

    def normalise(i, _):
        rows = part(i, 256)
        for s in range(2):
            lanes = slice(s * H, s * H + H)
            product = jnp.concatenate([bs[2, 0, rows, lanes], bs[2, 1, rows, lanes]], 1)
            new = dot_full(product, linv[0, s], NT)
            zb[0, rows, lanes] = new[:, 0:H]
            zb[1, rows, lanes] = new[:, H:K]
        return 0

    lax.fori_loop(0, 2, normalise, 0)

    squares(2, zb.at[0], zb.at[1])
    for half in range(2):
        project(2, half, zb.at[half])
    relay(2, [8, 9], [], [])
    relay(2, [10], [8], [])
    relay(2, [0], [9], [])
    relay(2, [1], [10], [8, 9, 10])
    factor = inverse_factor(tot.at[2, 8], tot.at[2, 9], tot.at[2, 10], linv.at[1, c])
    advance(factor, 2)
    for step in range(2, 8):
        relay(2, [step], [step - 2], [step - 2])
        advance(factor, 3)
    relay(2, [], [6], [6])
    advance(factor, 2)
    relay(2, [], [7], [7])
    for half in range(2):
        y3[half, part(c, 4)] = tot[2, 4 * half : 4 * half + 4]
        y_copy(half, c).start()
    advance(factor, 100)
    factor_copy(1, c).start()
    for half in range(2):
        y_copy(half, 1 - c).wait_recv()
    factor_copy(1, 1 - c).wait_recv()
    for s in range(2):
        lanes = slice(s * H, s * H + H)
        vectors = jnp.concatenate([zb[0, part(c, 256), lanes], zb[1, part(c, 256), lanes]], 1)
        high, low = split(dot_full(vectors, linv[1, s], NT))
        bh[s, 0:256, :] = high
        bl[s, 0:256, :] = low
        high, low = split(linv[1, s])
        bh[s, 256:512, :] = high
        bl[s, 256:512, :] = low

    def clean(r, _):
        s = slot_of(r)
        high, low = split(jnp.concatenate([y3[0, r], y3[1, r]], 1))
        coefficients = dot3(high, low, bh[s, 256:512, :], bl[s, 256:512, :], NT)
        high, low = split(coefficients)
        columns = part(r, 128)
        out[:, columns] = frames[:, columns] - dot3(bh[s, 0:256, :], bl[s, 0:256, :], high, low, NT)
        return 0

    lax.fori_loop(0, 8, clean, 0)

    x_copy(c).wait_send()
    base_copy(zh).wait_send()
    each_peer(lambda d: id_copy(d, q).wait_send())
    for half in range(2):
        y_copy(half, c).wait_send()
        factor_copy(half, c).wait_send()
        for phase in range(3):
            each_peer(lambda d: g_copy(phase, half, d, q).wait_send())
            half_copy(phase, half, c).wait_send()
        for phase in range(2):
            each_peer(lambda d: r_copy(phase, half, d, q).wait_send())
            p_copy(phase, half).wait_send()
    for phase in range(3):
        count = 11 if phase > 0 else 8

        @pl.when(is_mid)
        def _():
            def sent(ch, _):
                mid_copy(phase, ch).wait_send()
                total_copy(phase, ch).wait_send()
                return 0

            lax.fori_loop(0, count, sent, 0)

        @pl.when(is_end)
        def _():
            def sent(ch, _):
                end_copy(phase, ch).wait_send()
                return 0

            lax.fori_loop(0, count, sent, 0)


def solution(mesh):
    def step(frames, ann_rows, start_bases):
        vmem = pl.BlockSpec(memory_space=pltpu.VMEM)
        dma = pltpu.SemaphoreType.DMA
        return pl.pallas_call(
            kernel,
            out_shape=jax.ShapeDtypeStruct(frames.shape, F32),
            in_specs=[vmem, pl.BlockSpec(memory_space=pltpu.SMEM), vmem],
            out_specs=vmem,
            scratch_shapes=[
                pltpu.VMEM((512, 512), F32),
                pltpu.VMEM((512, 512), BF16),
                pltpu.VMEM((512, 512), BF16),
                pltpu.VMEM((512, 512), BF16),
                pltpu.VMEM((512, 512), BF16),
                pltpu.VMEM((3, 2, 512, K), F32),
                pltpu.VMEM((2, 512, K), BF16),
                pltpu.VMEM((2, 512, K), BF16),
                pltpu.VMEM((2, 512, K), F32),
                pltpu.VMEM((3, CHUNKS, 128, H), F32),
                pltpu.VMEM((3, CHUNKS, 128, H), F32),
                pltpu.VMEM((3, CHUNKS, 128, H), F32),
                pltpu.VMEM((3, CHUNKS, 128, H), F32),
                pltpu.VMEM((2, 512, K), BF16),
                pltpu.VMEM((2, 512, K), BF16),
                pltpu.VMEM((2, 2, 512, K), F32),
                pltpu.VMEM((2, 2, 256, K), F32),
                pltpu.VMEM((2, 2, 256, K), F32),
                pltpu.VMEM((2, 2, NPL, 16, K), F32),
                pltpu.VMEM((3, 2, ANN, 16, H), F32),
                pltpu.VMEM((2, 2, ANN, 16, H), F32),
                pltpu.VMEM((3, 2, NPL, 16, K), F32),
                pltpu.VMEM((8, K), jnp.int32),
                pltpu.VMEM((NPL, 8, K), jnp.int32),
                pltpu.VMEM((2, 2, K, K), F32),
                pltpu.VMEM((2, 8, 128, H), F32),
                pltpu.VMEM((2, ANN, 8, H), F32),
                dma((15,)), dma((15,)),
                dma((11, NPL)), dma((11, NPL)),
                dma((5,)), dma((5,)),
                dma((3, 3, CHUNKS)), dma((3, 3, CHUNKS)),
            ],
            compiler_params=pltpu.CompilerParams(
                collective_id=0, has_side_effects=True, vmem_limit_bytes=56 * 1024 * 1024
            ),
        )(frames, ann_rows, start_bases)

    return jax.shard_map(
        step,
        mesh=mesh,
        in_specs=(P("tm", "pix"), P("pix"), P(None, ("tm", "pix"), None)),
        out_specs=P("tm", "pix"),
        check_vma=False,
    )
```

time: 215 us -> 157 us (0.73)
  Pallas kernels: 213 us -> 154 us
    pallas_call x1, Pallas kernels: 213 us -> 154 us  [step(): pl.pallas_call(kernel, out_shape=jax.ShapeDtypeStruct(frames.shape, F32),...]
where the time goes in v2:
time: 157 us
  Pallas kernels  154 us (98%)
  local copies, waits for them, and re-layouts  2.31 us (1%)
    pallas_call x1, Pallas kernels, step(): pl.pallas_call(kernel, out_shape=jax.ShapeDtypeStruct(frames.shape, F32),...  154 us

profile of v2, /device:TPU:1, one launch (start us, length us, event | category | flops | bytes accessed | tf_op | source)
XLA Modules:
  0.0 156.8 jit_solution(362564996469192859)
XLA Ops:
  0.0 154.4 %shard_map.37 = f32[256,1024]{1,0:T(8,128)} custom-call(f32[256,1024]{1,0:T(8,128)} %frames.1, s32[8]{0:T(128)} %ids.1, f32[4,8,256]{2,1,0:T(8,128)} %base.1), custom_call_target="tpu_custom_call" | custom-call | tf_op jit(solution)/shard_map/pallas_call | solution.py:493
  154.5 2.3 %copy.5 = f32[256,1024]{1,0:T(8,128)} copy(f32[256,1024]{1,0:T(8,128)} %shard_map.37) | data formatting | bytes 2097152

commit v3 on v2

--- a/solution.py
+++ b/solution.py
@@ -95,12 +95,13 @@
 
 
 def kernel(
-    frames, ids, base, out,
+    frames_in, ids, base_in, out,
+    frames, base,
     xw, xh, xl, xth, xtl, bs, bh, bl, zb,
     own, erecv, mrecv, tot, ymh, yml,
     pbuf, prec, rsend, rrecv, st, zrecv, gbuf, idtile, idall,
-    linv, y3, base0,
-    core_send, core_recv, plane_send, plane_recv, zsend, zrec, line_send, line_recv,
+    linv, y3, base0, found,
+    local, core_send, core_recv, plane_send, plane_recv, zsend, zrec, line_send, line_recv,
 ):
     t, p = lax.axis_index("tm"), lax.axis_index("pix")
     c, zl = lax.rem(t, 2), t // 2
@@ -133,6 +134,10 @@
     def part(index, size):
         return pl.ds(pl.multiple_of(index * size, size), size)
 
+    fetch = pltpu.make_async_copy(frames_in, frames, local.at[8])
+    fetch.start()
+    fetch_base = pltpu.make_async_copy(base_in, base, local.at[9])
+    fetch_base.start()
     barrier = pltpu.get_barrier_semaphore()
     greet(other)
     greet(across)
@@ -147,12 +152,13 @@
     idtile[:, 0:H] = jnp.full((8, H), first_id, jnp.int32)
     idtile[:, H:K] = jnp.full((8, H), last_id, jnp.int32)
     idall[q] = idtile[...]
+    fetch_base.wait()
     for half in range(2):
         base0[half] = base[:, :, half * H : half * H + H]
     pl.semaphore_wait(barrier, jnp.where(is_mid, 19, 18))
 
-    def x_copy(side):
-        return remote(frames.at[:, part(1 - c, 512)], xw.at[part(side, 256), :], core_send.at[0], core_recv.at[0], other)
+    def x_copy():
+        return remote(frames.at[:, part(1 - c, 512)], xw, core_send.at[0], core_recv.at[0], other)
 
     def id_copy(d, src):
         return remote(idtile, idall.at[src], plane_send.at[0, d], plane_recv.at[0, src], peer(d))
@@ -206,15 +212,15 @@
             linv.at[which, slot], linv.at[which, slot], core_send.at[11 + which], core_recv.at[11 + which], other
         )
 
-    def y_copy(half, side):
-        rows = y3.at[half, part(side, 4)]
-        return remote(rows, rows, core_send.at[13 + half], core_recv.at[13 + half], other)
+    def y_copy(row, side):
+        rows = y3.at[4 * side + row]
+        return remote(rows, rows, core_send.at[13 + row], core_recv.at[13 + row], other)
 
     base_copy(zh).start()
+    fetch.wait()
+    x_copy().start()
     each_peer(lambda d: id_copy(d, q).start())
-    x_copy(c).start()
     st[0, :, :, part(zh, 8), :] = base0[...]
-    xw[part(c, 256), :] = frames[:, part(c, 512)]
 
     def slot_of(row):
         return jnp.where(ids[row] == first_id, 0, 1)
@@ -283,25 +289,28 @@
         own[phase, 10] = dot_full(turned, second)
         send_own(phase, 10)
 
-    def back(phase, half):
-        def mask(r, _):
-            rows = part(r, 128)
+    def back(phase, half, step):
+        for r in (2 * step, 2 * step + 1):
+            rows = slice(128 * r, 128 * r + 128)
             slot = slot_of(4 * c + r)
             value = tot[phase, 4 * half + r]
             high, low = split(jnp.concatenate([jnp.where(slot == 0, value, 0.0), jnp.where(slot == 1, value, 0.0)], 1))
             ymh[half, rows, :] = high
             yml[half, rows, :] = low
-            return 0
-
-        lax.fori_loop(0, 4, mask, 0)
+        depth = slice(256 * step, 256 * step + 256)
 
         def multiply(i, _):
             rows = part(i, 256)
-            pbuf[phase, half, rows, :] = dot3(xh[rows, :], xl[rows, :], ymh[half], yml[half])
+            product = dot3(xh[rows, depth], xl[rows, depth], ymh[half, depth, :], yml[half, depth, :])
+            if step == 0:
+                pbuf[phase, half, rows, :] = product
+            else:
+                pbuf[phase, half, rows, :] = pbuf[phase, half, rows, :] + product
             return 0
 
         lax.fori_loop(0, 2, multiply, 0)
-        p_copy(phase, half).start()
+        if step == 1:
+            p_copy(phase, half).start()
 
     def scatter(phase, half):
         p_copy(phase, half).wait_recv()
@@ -330,64 +339,76 @@
         z_copy(phase, half).wait()
         st[phase, half] = st[phase, half] + zrecv[phase - 1, half]
 
-    x_copy(1 - c).wait_recv()
-
-    def layouts(i, _):
-        rows = part(i, 128)
-        block = xw[rows, :]
+    def layout(block, rows):
         high, low = split(block)
         xh[rows, :] = high
         xl[rows, :] = low
         high, low = split(block.T)
         xth[:, rows] = high
         xtl[:, rows] = low
+
+    def layout_own(i, _):
+        layout(frames[part(i, 128), part(c, 512)], part(2 * c + i, 128))
         return 0
 
-    lax.fori_loop(0, 4, layouts, 0)
+    def layout_other(i, _):
+        layout(xw[part(i, 128), :], part(2 * (1 - c) + i, 128))
+        return 0
+
+    lax.fori_loop(0, 2, layout_own, 0)
+    x_copy().wait_recv()
+    lax.fori_loop(0, 2, layout_other, 0)
     base_copy(1 - zh).wait_recv()
     each_peer(lambda d: id_copy(d, d).wait_recv())
     for half in range(2):
         share(0, half)
 
+    def received(phase, half):
+        half_copy(phase, half, 1 - c).wait_recv()
+
     factor = iter(())
     for phase in range(2):
-        for half in range(2):
-            shared(phase, half)
-        for half in range(2):
-            half_copy(phase, half, 1 - c).wait_recv()
-            project(phase, half, bs.at[phase, half])
+        last = phase == 1
+        shared(phase, 0)
+        received(phase, 0)
+        project(phase, 0, bs.at[phase, 0])
+        shared(phase, 1)
         relay(phase, [0, 1], [], [])
-        if phase == 1:
+        received(phase, 1)
+        project(phase, 1, bs.at[phase, 1])
+        relay(phase, [2], [], [])
+        relay(phase, [3], [0], [])
+        if last:
             squares(1, bs.at[1, 0], bs.at[1, 1])
-        relay(phase, [2], [0], [])
-        relay(phase, [3], [1], [])
-        relay(phase, [4], [2], [])
-        relay(phase, [5], [3], [0, 1, 2, 3])
-        back(phase, 0)
-        relay(phase, [6], [4], [])
-        relay(phase, [7], [5], [])
-        if phase == 1:
-            relay(phase, [8], [6], [])
-            relay(phase, [9], [7], [4, 5, 6, 7])
-        else:
-            relay(phase, [], [6, 7], [4, 5, 6, 7])
-        back(phase, 1)
-        if phase == 1:
-            relay(phase, [10], [8], [])
+        relay(phase, [4], [1], [0, 1])
+        back(phase, 0, 0)
+        relay(phase, [5], [2], [])
+        relay(phase, [6], [3], [2, 3])
+        back(phase, 0, 1)
+        relay(phase, [7], [4], [])
+        relay(phase, [8] if last else [], [5], [])
         scatter(phase, 0)
-        if phase == 1:
-            relay(phase, [], [9, 10], [])
+        relay(phase, [9] if last else [], [6], [4, 5])
+        back(phase, 1, 0)
+        relay(phase, [10] if last else [], [7], [6, 7])
+        back(phase, 1, 1)
+        if last:
+            relay(1, [], [8], [])
+        combine(phase, 0)
+        if last:
+            relay(1, [], [9, 10], [])
         scatter(phase, 1)
-        if phase == 1:
-            relay(phase, [], [], [8, 9, 10])
+        if last:
+            relay(1, [], [], [8, 9, 10])
             factor = inverse_factor(tot.at[1, 8], tot.at[1, 9], tot.at[1, 10], linv.at[0, c])
-        advance(factor, 10)
-        for half in range(2):
-            combine(phase, half)
-        advance(factor, 10)
-        for half in range(2):
-            settle(phase + 1, half)
-            share(phase + 1, half)
+        advance(factor, 6)
+        settle(phase + 1, 0)
+        share(phase + 1, 0)
+        advance(factor, 6)
+        combine(phase, 1)
+        advance(factor, 8)
+        settle(phase + 1, 1)
+        share(phase + 1, 1)
         advance(factor, 100)
     factor_copy(0, c).start()
 
@@ -411,26 +432,40 @@
 
     squares(2, zb.at[0], zb.at[1])
     for half in range(2):
-        project(2, half, zb.at[half])
-    relay(2, [8, 9], [], [])
-    relay(2, [10], [8], [])
-    relay(2, [0], [9], [])
-    relay(2, [1], [10], [8, 9, 10])
+        high, low = split(zb[half])
+        bh[half] = high
+        bl[half] = low
+
+    def chunks(r, _):
+        rows = part(r, 128)
+        for half in range(2):
+            both = dot3(xth[rows, :], xtl[rows, :], bh[half], bl[half])
+            own[2, 4 * half + r] = jnp.where(slot_of(4 * c + r) == 0, both[:, 0:H], both[:, H:K])
+            send_own(2, 4 * half + r)
+        return 0
+
+    lax.fori_loop(0, 4, chunks, 0)
+    order = [8, 9, 10, 0, 4, 1, 5, 2, 6, 3, 7]
+    relay(2, order[0:2], [], [])
+    relay(2, order[2:3], [], [])
+    relay(2, order[3:4], order[0:1], order[0:3])
     factor = inverse_factor(tot.at[2, 8], tot.at[2, 9], tot.at[2, 10], linv.at[1, c])
-    advance(factor, 2)
-    for step in range(2, 8):
-        relay(2, [step], [step - 2], [step - 2])
+    for step in range(4, 11):
+        advance(factor, 4 if step > 5 else 2)
+        relay(2, order[step : step + 1], order[step - 3 : step - 2], [])
+    for step in range(8, 11):
         advance(factor, 3)
-    relay(2, [], [6], [6])
-    advance(factor, 2)
-    relay(2, [], [7], [7])
-    for half in range(2):
-        y3[half, part(c, 4)] = tot[2, 4 * half : 4 * half + 4]
-        y_copy(half, c).start()
+        relay(2, [], order[step : step + 1], [])
     advance(factor, 100)
     factor_copy(1, c).start()
-    for half in range(2):
-        y_copy(half, 1 - c).wait_recv()
+
+    def deliver(row):
+        relay(2, [], [], [row, 4 + row])
+        y3[4 * c + row] = jnp.concatenate([tot[2, row], tot[2, 4 + row]], 1)
+        y_copy(row, c).start()
+
+    for row in range(3):
+        deliver(row)
     factor_copy(1, 1 - c).wait_recv()
     for s in range(2):
         lanes = slice(s * H, s * H + H)
@@ -442,22 +477,36 @@
         bh[s, 256:512, :] = high
         bl[s, 256:512, :] = low
 
-    def clean(r, _):
+    def out_copy(r):
+        columns = part(r, 128)
+        return pltpu.make_async_copy(found.at[:, columns], out.at[:, columns], local.at[r])
+
+    def clean(r):
         s = slot_of(r)
-        high, low = split(jnp.concatenate([y3[0, r], y3[1, r]], 1))
+        high, low = split(y3[r])
         coefficients = dot3(high, low, bh[s, 256:512, :], bl[s, 256:512, :], NT)
         high, low = split(coefficients)
-        columns = part(r, 128)
-        out[:, columns] = frames[:, columns] - dot3(bh[s, 0:256, :], bl[s, 0:256, :], high, low, NT)
+        found[:, part(r, 128)] = dot3(bh[s, 0:256, :], bl[s, 0:256, :], high, low, NT)
+        out_copy(r).start()
+
+    def clean_both(row, _):
+        clean(4 * c + row)
+        y_copy(row, 1 - c).wait_recv()
+        clean(4 * (1 - c) + row)
         return 0
 
-    lax.fori_loop(0, 8, clean, 0)
-
-    x_copy(c).wait_send()
+    lax.fori_loop(0, 3, clean_both, 0)
+    deliver(3)
+    clean_both(3, 0)
+
+    for r in range(8):
+        out_copy(r).wait()
+    x_copy().wait_send()
     base_copy(zh).wait_send()
     each_peer(lambda d: id_copy(d, q).wait_send())
+    for row in range(4):
+        y_copy(row, c).wait_send()
     for half in range(2):
-        y_copy(half, c).wait_send()
         factor_copy(half, c).wait_send()
         for phase in range(3):
             each_peer(lambda d: g_copy(phase, half, d, q).wait_send())
@@ -488,15 +537,17 @@
 
 def solution(mesh):
     def step(frames, ann_rows, start_bases):
-        vmem = pl.BlockSpec(memory_space=pltpu.VMEM)
+        anywhere = pl.BlockSpec(memory_space=pl.ANY)
         dma = pltpu.SemaphoreType.DMA
-        return pl.pallas_call(
+        found = pl.pallas_call(
             kernel,
             out_shape=jax.ShapeDtypeStruct(frames.shape, F32),
-            in_specs=[vmem, pl.BlockSpec(memory_space=pltpu.SMEM), vmem],
-            out_specs=vmem,
+            in_specs=[pl.BlockSpec(memory_space=pltpu.HBM), pl.BlockSpec(memory_space=pltpu.SMEM), pl.BlockSpec(memory_space=pltpu.HBM)],
+            out_specs=anywhere,
             scratch_shapes=[
-                pltpu.VMEM((512, 512), F32),
+                pltpu.VMEM((256, 1024), F32),
+                pltpu.VMEM((ANN, 8, K), F32),
+                pltpu.VMEM((256, 512), F32),
                 pltpu.VMEM((512, 512), BF16),
                 pltpu.VMEM((512, 512), BF16),
                 pltpu.VMEM((512, 512), BF16),
@@ -521,17 +572,20 @@
                 pltpu.VMEM((8, K), jnp.int32),
                 pltpu.VMEM((NPL, 8, K), jnp.int32),
                 pltpu.VMEM((2, 2, K, K), F32),
-                pltpu.VMEM((2, 8, 128, H), F32),
+                pltpu.VMEM((8, 128, K), F32),
                 pltpu.VMEM((2, ANN, 8, H), F32),
-                dma((15,)), dma((15,)),
+                pltpu.VMEM((256, 1024), F32),
+                dma((10,)),
+                dma((17,)), dma((17,)),
                 dma((11, NPL)), dma((11, NPL)),
                 dma((5,)), dma((5,)),
                 dma((3, 3, CHUNKS)), dma((3, 3, CHUNKS)),
             ],
             compiler_params=pltpu.CompilerParams(
-                collective_id=0, has_side_effects=True, vmem_limit_bytes=56 * 1024 * 1024
+                collective_id=0, has_side_effects=True, vmem_limit_bytes=52 * 1024 * 1024
             ),
         )(frames, ann_rows, start_bases)
+        return frames - found
 
     return jax.shard_map(
         step,

time: 157 us -> 143 us (0.911)
  Pallas kernels: 154 us -> 141 us
    pallas_call x1, Pallas kernels: 154 us -> 141 us  [step(): pl.pallas_call(kernel, out_shape=jax.ShapeDtypeStruct(frames.shape, F32),...]
where the time goes in v3:
time: 143 us
  Pallas kernels  141 us (99%)
    pallas_call x1, Pallas kernels, step(): pl.pallas_call(kernel, out_shape=jax.ShapeDtypeStruct(frames.shape, F32),...  141 us

profile of v3, /device:TPU:1, one launch (start us, length us, event | category | flops | bytes accessed | tf_op | source)
XLA Modules:
  0.0 143.1 jit_solution(5690541131725383439)
XLA Ops:
  0.0 0.0 copy-start
  0.0 0.8 copy-done
  0.8 0.0 copy-start.1
  0.8 0.7 copy-done.1
  1.4 0.0 copy-start.2
  1.4 140.5 %shard_map.37 = f32[256,1024]{1,0:T(8,128)S(1)} custom-call(f32[256,1024]{1,0:T(8,128)} %frames_in.1, s32[8]{0:T(128)S(1)} %copy-done.1, f32[4,8,256]{2,1,0:T(8,128)S(1)} %copy-done), custom_call_target="tpu_custom_call" | custom-call | tf_op jit(solution)/shard_map/pallas_call | solution.py:542
  141.9 0.0 copy-done.2
  142.0 1.1 sub.3
Async XLA Ops:
  0.0 0.8 copy-start
  0.8 0.7 copy-start.1
  1.4 140.5 %copy-start.2 = (f32[256,1024]{1,0:T(8,128)S(1)}, f32[256,1024]{1,0:T(8,128)}, u32[]{:S(2)}) copy-start(f32[256,1024]{1,0:T(8,128)} %frames_in.1) | copy-start | bytes 3145732
